TPU v7x, 32 devices: a whole 2x2x4 slice. The times are simulated.
32 devices in a mesh: dp: 16 (over z, x, core), mp: 2 (over y).
Axes of the slice: x: 2, y: 2, z: 4, core: 2. Of those that a mesh axis runs over, the one named last changes fastest.
Arguments:
- tokens: bfloat16 [16, 1024, 3584], P('dp'), may hold values from -14 to 14
- modality: int32 [16, 8], P('dp'), may hold values from 0 to 1, as said below
- block_mask: int32 [16, 8, 8], P('dp'), may hold values from 0 to 2, as said below
- q_weight: bfloat16 [2, 3584, 2048], P(None, 'dp', 'mp'), may hold values from -0.09375 to 0.09375
- kv_weight: bfloat16 [2, 3584, 1024], P(None, 'dp'), may hold values from -0.09375 to 0.09375
- o_weight: bfloat16 [2, 2048, 3584], P(None, 'mp', 'dp'), may hold values from -0.125 to 0.125
Outputs:
- attn_out: bfloat16 [16, 1024, 3584], P('dp', 'mp')
Inputs may be any that keep to these rules, and one draw needn't show every extreme that they name: modality[s, b] names the section (0 text, 1 image) whose weights serve the 128 tokens of block b of sequence s. block_mask[s, i, j] tells which tokens of block i see block j: 0 none, 1 all, 2 those at or before the query's position; every diagonal entry is 1 or 2, every entry off the diagonal is 0 or 1.
All inputs are finite; a program needn't handle non-finite values.
Results may differ from a plain program's by a relative error of at most 0.015.
Values may be sent and summed in bfloat16 or wider, within the bound.
A program may use at most 128 MiB of HBM per device.

v0:
```python
import jax
import jax.numpy as jnp
from jax import lax
from jax.sharding import PartitionSpec as P

HD = 128
KVH = 4
QHEADS = 16
BLK = 128


rope_theta = 1000000.0


def rotary_tables(length, head_width):
    half_width = head_width // 2
    frequency = rope_theta ** (-jnp.arange(half_width, dtype=jnp.float32) * 2.0 / head_width)
    angles = jnp.arange(length, dtype=jnp.float32)[:, None] * frequency[None, :]
    angles = jnp.concatenate([angles, angles], axis=1)
    return (jnp.cos(angles), jnp.sin(angles))


def rotate(values, cosine_table, sine_table):
    half_width = values.shape[-1] // 2
    turned = jnp.concatenate([-values[..., half_width:], values[..., :half_width]], axis=-1)
    return values * cosine_table[:, None, :] + turned * sine_table[:, None, :]


def project_rows(blocks, block_kinds, pieces):

    def one_block(inputs):
        row_block, block_kind = inputs
        return tuple(
            (
                jnp.dot(
                    row_block,
                    lax.dynamic_index_in_dim(shard_piece, block_kind, 0, keepdims=False),
                    preferred_element_type=jnp.float32,
                )
                for shard_piece in pieces
            )
        )

    products = lax.map(one_block, (blocks, block_kinds))
    return tuple((product for product in products))


def local(tokens, modality, block_mask, q_weight, kv_weight, o_weight):
    states = tokens[0]
    block_kinds = modality[0]
    layout = block_mask[0]
    length = states.shape[0]
    model_width = states.shape[1]
    block_count = length // BLK
    blocks = states.reshape(block_count, BLK, model_width)
    head_cols = q_weight.shape[2]
    local_heads = head_cols // HD
    group_size = QHEADS // KVH
    pair_heads = max(1, local_heads // group_size)
    pair_cols = pair_heads * 2 * HD
    model_index = lax.axis_index("mp")
    first_pair = model_index * local_heads // group_size
    kv_needed = lax.dynamic_slice_in_dim(kv_weight, first_pair * (2 * HD), pair_cols, 2)
    query_sum, pair_sum = project_rows(
        blocks,
        block_kinds,
        (
            lax.all_gather(q_weight, "dp", axis=1, tiled=True),
            lax.all_gather(kv_needed, "dp", axis=1, tiled=True),
        ),
    )
    cosine_table, sine_table = rotary_tables(length, HD)
    queries = rotate(query_sum.reshape(length, local_heads, HD), cosine_table, sine_table).astype(
        jnp.bfloat16
    )
    pair_raw = pair_sum.reshape(length, pair_heads, 2, HD)
    key_heads = rotate(pair_raw[:, :, 0], cosine_table, sine_table).astype(jnp.bfloat16)
    value_heads = pair_raw[:, :, 1].astype(jnp.bfloat16)
    queries = queries.reshape(length, pair_heads, local_heads // pair_heads, HD)
    block_rows = min(512, length)
    score_scale = HD ** (-0.5)
    positions = jnp.arange(length, dtype=jnp.int32)

    def attend(block_index):
        first_row = block_index * block_rows
        query_part = lax.dynamic_slice_in_dim(queries, first_row, block_rows, 0)
        rows_mask = lax.dynamic_slice_in_dim(layout, first_row // BLK, block_rows // BLK, 0)
        expanded = jnp.broadcast_to(
            rows_mask[:, None, :, None], (block_rows // BLK, BLK, block_count, BLK)
        ).reshape(block_rows, length)
        query_pos = first_row + jnp.arange(block_rows, dtype=jnp.int32)
        allowed = (expanded == 1) | (expanded == 2) & (positions[None, :] <= query_pos[:, None])
        scores = (
            jnp.einsum("qgjd,kgd->gjqk", query_part, key_heads, preferred_element_type=jnp.float32)
            * score_scale
        )
        scores = jnp.where(allowed[None, None], scores, -1e30)
        row_max = jnp.max(scores, axis=-1, keepdims=True)
        weights = jnp.exp(scores - row_max)
        weights = (weights / jnp.sum(weights, axis=-1, keepdims=True)).astype(jnp.bfloat16)
        mixed_out = jnp.einsum(
            "gjqk,kgd->qgjd", weights, value_heads, preferred_element_type=jnp.float32
        )
        return mixed_out.astype(jnp.bfloat16).reshape(block_rows, head_cols)

    attended_flat = lax.map(attend, jnp.arange(length // block_rows, dtype=jnp.int32)).reshape(
        length, head_cols
    )
    out_full = lax.all_gather(o_weight, "dp", axis=2, tiled=True)
    row_kinds = jnp.repeat(block_kinds, BLK)
    text_part = jnp.dot(attended_flat, out_full[0], preferred_element_type=jnp.float32)
    image_part = jnp.dot(attended_flat, out_full[1], preferred_element_type=jnp.float32)
    summed = lax.psum_scatter(
        jnp.where(row_kinds[:, None] == 1, image_part, text_part).astype(jnp.bfloat16),
        "mp",
        scatter_dimension=0,
        tiled=True,
    )
    return summed[None]


def solution(mesh):
    in_specs = (
        P("dp", None, None),
        P("dp", None),
        P("dp", None, None),
        P(None, "dp", "mp"),
        P(None, "dp", None),
        P(None, "mp", "dp"),
    )
    out_specs = P("dp", "mp", None)
    return jax.shard_map(local, mesh=mesh, in_specs=in_specs, out_specs=out_specs, check_vma=False)
```

profile of v0, /device:TPU:0, one launch (start us, length us, event | category | flops | bytes accessed | tf_op | source)
XLA Modules:
  0.0 492.2 jit_solution(15514788760699817626)
XLA Ops:
  6.5 1.2 copy-done
  7.7 0.8 constant_dynamic-slice_fusion
  10.3 1.9 fusion.64
  12.8 67.9 %all-gather.6.cloned.1.call-done = bf16[2,3584,512]{2,1,0:T(8,128)(2,1)} async-done(((bf16[2,224,512]{2,1,0:T(8,128)(2,1)}), bf16[2,3584,512]{2,1,0:T(8,128)(2,1)}) %all-gather.6.cloned.1.call-update) | async-done | bytes 7340048 | tf_op jit(solution)/shard_map/all_gather | solution.py:69
  80.7 114.6 %all-gather.4.cloned.1.call-done = bf16[2,3584,1024]{2,1,0:T(8,128)(2,1)} async-done(((bf16[2,224,1024]{2,1,0:T(8,128)(2,1)}), bf16[2,3584,1024]{2,1,0:T(8,128)(2,1)}) %all-gather.4.cloned.1.call-update) | async-done | bytes 14680080 | tf_op jit(solution)/shard_map/all_gather | solution.py:68
  195.3 88.1 %while.25 = (s32[]{:T(128)}, f32[8,128,1024]{2,1,0:T(8,128)}, f32[8,128,512]{2,1,0:T(8,128)}, bf16[8,128,3584]{2,1,0:T(8,128)(2,1)}, s32[8]{0:T(128)S(1)}, /*ind...) while((s32[]{:T(128)}, f32[8,128,1024]{2,1,0:T(8,128)}, ...), condition=%wide.region_1.2_spmd, body=%wide.region_0.1_spmd.sunk | while | flops 1409286144 | bytes 42993844 | solution.py:44
  198.0 5.4 %fusion.93 = f32[8,128,1024]{2,1,0:T(8,128)} fusion(f32[8,128,1024]{2,1,0:T(8,128)} %get-tuple-element.321, s32[]{:T(128)} %get-tuple-element.320, bf16[2,3584,1024]{2,1,0:T(8,128)(2,1)} %get-tuple-element.335, s32[]{:T(128)S(6)} %select_n.72, bf16[8,128,3584]{2,1,0:T(8,128)(2,1)} %get-tuple-element.333), kind=kOutput, calls=%fused_computation.8.clone.1 | convolution fusion | flops 939524096 | bytes 8782852 | tf_op jit(solution)/shard_map/while/body/eval_jaxpr/dot_general | solution.py:35
  203.7 2.6 fusion.94
  209.0 5.5 %fusion.93 = f32[8,128,1024]{2,1,0:T(8,128)} fusion(f32[8,128,1024]{2,1,0:T(8,128)} %get-tuple-element.321, s32[]{:T(128)} %get-tuple-element.320, bf16[2,3584,1024]{2,1,0:T(8,128)(2,1)} %get-tuple-element.335, s32[]{:T(128)S(6)} %select_n.72, bf16[8,128,3584]{2,1,0:T(8,128)(2,1)} %get-tuple-element.333), kind=kOutput, calls=%fused_computation.8.clone.1 | convolution fusion | flops 939524096 | bytes 8782852 | tf_op jit(solution)/shard_map/while/body/eval_jaxpr/dot_general | solution.py:35
  214.5 2.5 fusion.94
  219.7 5.5 %fusion.93 = f32[8,128,1024]{2,1,0:T(8,128)} fusion(f32[8,128,1024]{2,1,0:T(8,128)} %get-tuple-element.321, s32[]{:T(128)} %get-tuple-element.320, bf16[2,3584,1024]{2,1,0:T(8,128)(2,1)} %get-tuple-element.335, s32[]{:T(128)S(6)} %select_n.72, bf16[8,128,3584]{2,1,0:T(8,128)(2,1)} %get-tuple-element.333), kind=kOutput, calls=%fused_computation.8.clone.1 | convolution fusion | flops 939524096 | bytes 8782852 | tf_op jit(solution)/shard_map/while/body/eval_jaxpr/dot_general | solution.py:35
  225.3 2.5 fusion.94
  230.5 5.4 %fusion.93 = f32[8,128,1024]{2,1,0:T(8,128)} fusion(f32[8,128,1024]{2,1,0:T(8,128)} %get-tuple-element.321, s32[]{:T(128)} %get-tuple-element.320, bf16[2,3584,1024]{2,1,0:T(8,128)(2,1)} %get-tuple-element.335, s32[]{:T(128)S(6)} %select_n.72, bf16[8,128,3584]{2,1,0:T(8,128)(2,1)} %get-tuple-element.333), kind=kOutput, calls=%fused_computation.8.clone.1 | convolution fusion | flops 939524096 | bytes 8782852 | tf_op jit(solution)/shard_map/while/body/eval_jaxpr/dot_general | solution.py:35
  235.9 2.5 fusion.94
  241.2 7.3 %fusion.93 = f32[8,128,1024]{2,1,0:T(8,128)} fusion(f32[8,128,1024]{2,1,0:T(8,128)} %get-tuple-element.321, s32[]{:T(128)} %get-tuple-element.320, bf16[2,3584,1024]{2,1,0:T(8,128)(2,1)} %get-tuple-element.335, s32[]{:T(128)S(6)} %select_n.72, bf16[8,128,3584]{2,1,0:T(8,128)(2,1)} %get-tuple-element.333), kind=kOutput, calls=%fused_computation.8.clone.1 | convolution fusion | flops 939524096 | bytes 8782852 | tf_op jit(solution)/shard_map/while/body/eval_jaxpr/dot_general | solution.py:35
  248.4 2.5 fusion.94
  253.7 5.6 %fusion.93 = f32[8,128,1024]{2,1,0:T(8,128)} fusion(f32[8,128,1024]{2,1,0:T(8,128)} %get-tuple-element.321, s32[]{:T(128)} %get-tuple-element.320, bf16[2,3584,1024]{2,1,0:T(8,128)(2,1)} %get-tuple-element.335, s32[]{:T(128)S(6)} %select_n.72, bf16[8,128,3584]{2,1,0:T(8,128)(2,1)} %get-tuple-element.333), kind=kOutput, calls=%fused_computation.8.clone.1 | convolution fusion | flops 939524096 | bytes 8782852 | tf_op jit(solution)/shard_map/while/body/eval_jaxpr/dot_general | solution.py:35
  259.3 2.5 fusion.94
  264.5 5.6 %fusion.93 = f32[8,128,1024]{2,1,0:T(8,128)} fusion(f32[8,128,1024]{2,1,0:T(8,128)} %get-tuple-element.321, s32[]{:T(128)} %get-tuple-element.320, bf16[2,3584,1024]{2,1,0:T(8,128)(2,1)} %get-tuple-element.335, s32[]{:T(128)S(6)} %select_n.72, bf16[8,128,3584]{2,1,0:T(8,128)(2,1)} %get-tuple-element.333), kind=kOutput, calls=%fused_computation.8.clone.1 | convolution fusion | flops 939524096 | bytes 8782852 | tf_op jit(solution)/shard_map/while/body/eval_jaxpr/dot_general | solution.py:35
  270.1 2.6 fusion.94
  275.4 5.5 %fusion.93 = f32[8,128,1024]{2,1,0:T(8,128)} fusion(f32[8,128,1024]{2,1,0:T(8,128)} %get-tuple-element.321, s32[]{:T(128)} %get-tuple-element.320, bf16[2,3584,1024]{2,1,0:T(8,128)(2,1)} %get-tuple-element.335, s32[]{:T(128)S(6)} %select_n.72, bf16[8,128,3584]{2,1,0:T(8,128)(2,1)} %get-tuple-element.333), kind=kOutput, calls=%fused_computation.8.clone.1 | convolution fusion | flops 939524096 | bytes 8782852 | tf_op jit(solution)/shard_map/while/body/eval_jaxpr/dot_general | solution.py:35
  280.8 2.5 fusion.94
  283.4 2.6 reshape.136
  285.9 1.8 slice.35
  287.7 2.1 slice.38
  289.7 2.3 copy.28
  292.5 1.0 copy.17
  293.6 5.6 %reshape.135 = f32[1024,2,4,128]{3,2,1,0:T(4,128)} reshape(f32[8,128,1024]{2,1,0:T(8,128)} %get-tuple-element.145) | data formatting | bytes 8388608 | tf_op jit(solution)/shard_map/reshape | solution.py:73
  299.2 3.2 copy.32
  302.4 4.7 fusion.74
  307.1 3.0 copy.26
  310.1 1.5 neg.16
  311.6 2.8 copy.27
  314.5 5.3 %copy.21 = f32[1024,2,4,128]{0,3,2,1:T(8,128)} copy(f32[1024,2,4,128]{3,2,1,0:T(4,128)} %reshape.135) | data formatting | bytes 8388608 | tf_op jit(solution)/shard_map/reshape | solution.py:73
  319.7 3.5 copy.29
  323.2 5.4 %fusion.60 = bf16[1024,2,4,128]{0,3,2,1:T(8,128)(2,1)} fusion(f32[1024,2,4,64]{0,3,2,1:T(8,128)S(1)} %bitcast.134, f32[1024,2,4,64]{0,3,2,1:T(8,128)} %bitcast.135, f32[1024,2,4,128]{0,3,2,1:T(8,128)} %copy.21, f32[1024,128]{0,1:T(8,128)S(1)} %get-tuple-element.215, f32[1024,128]{0,1:T(8,128)S(1)} %get-tuple-element.214), kind=kLoop, calls=%fused_computation.53 | loop fusion | flops 5242880 | bytes 11534336 | tf_op jit(solution)/shard_map/convert_element_type | solution.py:73
  328.6 44.8 %while.26 = (s32[]{:T(128)}, bf16[2,512,1024]{2,1,0:T(8,128)(2,1)}, s32[2]{0:T(128)S(1)}, s32[8,8]{1,0:T(8,128)S(1)}, bf16[1024,2,4,128]{0,3,2,1:T(8,128)(2,1)},...) while((s32[]{:T(128)}, bf16[2,512,1024]{2,1,0:T(8,128)(2,1)}, ...), condition=%wide.region_5.6_spmd.clone, body=%wide.region_2.5_spmd.clone.sunk | while | flops 2174748160 | bytes 46175388 | solution.py:106
  330.4 0.7 fusion.98
  331.2 10.8 %fusion.99 = (f32[2,4,512]{2,1,0:T(4,128)S(1)}, f32[2,4,512,1024]{3,2,1,0:T(8,128)}) fusion(pred[512,1024]{1,0:T(8,128)(4,1)S(1)} %fusion.98, bf16[1024,2,4,128]{0,3,2,1:T(8,128)(2,1)} %get-tuple-element.374, s32[]{:T(128)S(6)} %select_n.76, bf16[1024,2,128]{2,0,1:T(8,128)(2,1)} %get-tuple-element.375), kind=kOutput, calls=%fused_computation.67.clone.1 | convolution fusion | flops 1090520064 | bytes 18890756 | tf_op jit(solution)/shard_map/while/body/eval_jaxpr/sub | solution.py:99
  342.0 7.4 %fusion.100 = bf16[2,4,512,128]{2,3,1,0:T(8,128)(2,1)S(1)} fusion(f32[2,4,512,1024]{3,2,1,0:T(8,128)} %get-tuple-element.308, f32[2,4,512]{2,1,0:T(4,128)S(1)} %get-tuple-element.309, bf16[1024,2,128]{0,2,1:T(8,128)(2,1)S(1)} %copy-done.3), kind=kOutput, calls=%fused_computation.32.clone.1 | convolution fusion | flops 1082654720 | bytes 18366464 | tf_op jit(solution)/shard_map/while/body/eval_jaxpr/gjqk,kgd->qgjd/dot_general | solution.py:101
  349.9 1.0 constant_dynamic-update-slice_fusion.2
  352.8 0.7 fusion.98
  353.5 10.8 %fusion.99 = (f32[2,4,512]{2,1,0:T(4,128)S(1)}, f32[2,4,512,1024]{3,2,1,0:T(8,128)}) fusion(pred[512,1024]{1,0:T(8,128)(4,1)S(1)} %fusion.98, bf16[1024,2,4,128]{0,3,2,1:T(8,128)(2,1)} %get-tuple-element.374, s32[]{:T(128)S(6)} %select_n.76, bf16[1024,2,128]{2,0,1:T(8,128)(2,1)} %get-tuple-element.375), kind=kOutput, calls=%fused_computation.67.clone.1 | convolution fusion | flops 1090520064 | bytes 18890756 | tf_op jit(solution)/shard_map/while/body/eval_jaxpr/sub | solution.py:99
  364.4 7.4 %fusion.100 = bf16[2,4,512,128]{2,3,1,0:T(8,128)(2,1)S(1)} fusion(f32[2,4,512,1024]{3,2,1,0:T(8,128)} %get-tuple-element.308, f32[2,4,512]{2,1,0:T(4,128)S(1)} %get-tuple-element.309, bf16[1024,2,128]{0,2,1:T(8,128)(2,1)S(1)} %copy-done.3), kind=kOutput, calls=%fused_computation.32.clone.1 | convolution fusion | flops 1082654720 | bytes 18366464 | tf_op jit(solution)/shard_map/while/body/eval_jaxpr/gjqk,kgd->qgjd/dot_general | solution.py:101
  372.3 1.0 constant_dynamic-update-slice_fusion.2
  373.4 12.7 %fusion.58 = bf16[1024,3584]{1,0:T(8,128)(2,1)} fusion(bf16[1024,1024]{1,0:T(8,128)(2,1)} %bitcast.138, bf16[2,1024,3584]{1,2,0:T(8,128)(2,1)} %all-gather.8.cloned.1.call-done), kind=kOutput, calls=%fused_computation.50 | convolution fusion | flops 7516192768 | bytes 16777216 | tf_op jit(solution)/shard_map/dot_general | solution.py:112
  386.1 12.7 %select_convert_fusion = bf16[1024,3584]{1,0:T(8,128)(2,1)} fusion(bf16[1024,3584]{1,0:T(8,128)(2,1)} %fusion.58, bf16[1024,1024]{1,0:T(8,128)(2,1)} %bitcast.139, bf16[2,1024,3584]{1,2,0:T(8,128)(2,1)S(1)} %copy-done.5, pred[1024]{0:T(1024)(128)(4,1)S(1)} %copy-done.7), kind=kOutput, calls=%fused_computation.47 | convolution fusion | flops 7519862784 | bytes 24118272 | tf_op jit(solution)/shard_map/dot_general | solution.py:111
  398.8 86.8 %reduce-scatter.2.cloned.1.call-done = bf16[512,3584]{1,0:T(8,128)(2,1)} async-done(((bf16[1024,3584]{1,0:T(8,128)(2,1)}), bf16[512,3584]{1,0:T(8,128)(2,1)}) %reduce-scatter.2.cloned.1.call-update) | async-done | bytes 3670032 | tf_op jit(solution)/shard_map/reduce_scatter | solution.py:113
  (70 shorter events, 11.5 us)
Async XLA Ops:
  6.5 1.2 copy-start
  6.5 5.6 %copy-start.6 = (s32[1,8]{1,0:T(1,128)S(1)}, s32[1,8]{1,0:T(1,128)}, u32[]{:S(2)}) copy-start(s32[1,8]{1,0:T(1,128)} %param.11) | copy-start | bytes 100
  6.5 74.1 %all-gather.6.cloned.1.call-start = ((), (), s32[]{:S(2)}) async-start(), calls=%async_computation.2 | async-start | bytes 7798784 | tf_op jit(solution)/shard_map/all_gather | solution.py:69
  8.6 186.7 %all-gather.4.cloned.1.call-start = ((), (), s32[]{:S(2)}) async-start(), calls=%async_computation.1 | async-start | bytes 15597568 | tf_op jit(solution)/shard_map/all_gather | solution.py:68
  9.3 364.0 %all-gather.8.cloned.1.call-start = ((), (), s32[]{:S(2)}) async-start(), calls=%async_computation.3 | async-start | bytes 15597568 | tf_op jit(solution)/shard_map/all_gather | solution.py:109
  10.1 475.6 %reduce-scatter.2.cloned.1.call-start = ((), (), s32[]{:S(2)}) async-start(), calls=%async_computation.4 | async-start | bytes 11010048 | tf_op jit(solution)/shard_map/reduce_scatter | solution.py:113
  198.0 5.7 %copy-start.2 = (bf16[2,3584,512]{2,1,0:T(8,128)(2,1)S(1)}, bf16[2,3584,512]{2,1,0:T(8,128)(2,1)}, u32[]{:S(2)}) copy-start(bf16[2,3584,512]{2,1,0:T(8,128)(2,1)} %get-tuple-element.336) | copy-start | bytes 22020100 | tf_op jit(solution)/shard_map/while
  209.0 5.5 %copy-start.2 = (bf16[2,3584,512]{2,1,0:T(8,128)(2,1)S(1)}, bf16[2,3584,512]{2,1,0:T(8,128)(2,1)}, u32[]{:S(2)}) copy-start(bf16[2,3584,512]{2,1,0:T(8,128)(2,1)} %get-tuple-element.336) | copy-start | bytes 22020100 | tf_op jit(solution)/shard_map/while
  219.7 5.5 %copy-start.2 = (bf16[2,3584,512]{2,1,0:T(8,128)(2,1)S(1)}, bf16[2,3584,512]{2,1,0:T(8,128)(2,1)}, u32[]{:S(2)}) copy-start(bf16[2,3584,512]{2,1,0:T(8,128)(2,1)} %get-tuple-element.336) | copy-start | bytes 22020100 | tf_op jit(solution)/shard_map/while
  230.5 5.4 %copy-start.2 = (bf16[2,3584,512]{2,1,0:T(8,128)(2,1)S(1)}, bf16[2,3584,512]{2,1,0:T(8,128)(2,1)}, u32[]{:S(2)}) copy-start(bf16[2,3584,512]{2,1,0:T(8,128)(2,1)} %get-tuple-element.336) | copy-start | bytes 22020100 | tf_op jit(solution)/shard_map/while
  241.2 7.3 %copy-start.2 = (bf16[2,3584,512]{2,1,0:T(8,128)(2,1)S(1)}, bf16[2,3584,512]{2,1,0:T(8,128)(2,1)}, u32[]{:S(2)}) copy-start(bf16[2,3584,512]{2,1,0:T(8,128)(2,1)} %get-tuple-element.336) | copy-start | bytes 22020100 | tf_op jit(solution)/shard_map/while
  253.7 5.6 %copy-start.2 = (bf16[2,3584,512]{2,1,0:T(8,128)(2,1)S(1)}, bf16[2,3584,512]{2,1,0:T(8,128)(2,1)}, u32[]{:S(2)}) copy-start(bf16[2,3584,512]{2,1,0:T(8,128)(2,1)} %get-tuple-element.336) | copy-start | bytes 22020100 | tf_op jit(solution)/shard_map/while
  264.5 5.6 %copy-start.2 = (bf16[2,3584,512]{2,1,0:T(8,128)(2,1)S(1)}, bf16[2,3584,512]{2,1,0:T(8,128)(2,1)}, u32[]{:S(2)}) copy-start(bf16[2,3584,512]{2,1,0:T(8,128)(2,1)} %get-tuple-element.336) | copy-start | bytes 22020100 | tf_op jit(solution)/shard_map/while
  275.3 5.5 %copy-start.2 = (bf16[2,3584,512]{2,1,0:T(8,128)(2,1)S(1)}, bf16[2,3584,512]{2,1,0:T(8,128)(2,1)}, u32[]{:S(2)}) copy-start(bf16[2,3584,512]{2,1,0:T(8,128)(2,1)} %get-tuple-element.336) | copy-start | bytes 22020100 | tf_op jit(solution)/shard_map/while
  323.2 5.4 %copy-start.4 = (s32[1,8,8]{2,1,0:T(8,128)S(1)}, s32[1,8,8]{2,1,0:T(8,128)}, u32[]{:S(2)}) copy-start(s32[1,8,8]{2,1,0:T(8,128)} %param.12) | copy-start | bytes 772
  331.1 10.8 %copy-start.3 = (bf16[1024,2,128]{0,2,1:T(8,128)(2,1)S(1)}, bf16[1024,2,128]{0,2,1:T(8,128)(2,1)}, u32[]{:S(2)}) copy-start(bf16[1024,2,128]{0,2,1:T(8,128)(2,1)} %get-tuple-element.376) | copy-start | bytes 1572868 | tf_op jit(solution)/shard_map/while
  353.5 10.8 %copy-start.3 = (bf16[1024,2,128]{0,2,1:T(8,128)(2,1)S(1)}, bf16[1024,2,128]{0,2,1:T(8,128)(2,1)}, u32[]{:S(2)}) copy-start(bf16[1024,2,128]{0,2,1:T(8,128)(2,1)} %get-tuple-element.376) | copy-start | bytes 1572868 | tf_op jit(solution)/shard_map/while
  373.4 12.7 %copy-start.5 = (bf16[2,1024,3584]{1,2,0:T(8,128)(2,1)S(1)}, bf16[2,1024,3584]{1,2,0:T(8,128)(2,1)}, u32[]{:S(2)}) copy-start(bf16[2,1024,3584]{1,2,0:T(8,128)(2,1)} %all-gather.8.cloned.1.call-done) | copy-start | bytes 44040196
  373.4 12.7 %copy-start.7 = (pred[1024]{0:T(1024)(128)(4,1)S(1)}, pred[1024]{0:T(1024)(128)(4,1)}, u32[]{:S(2)}) copy-start(pred[1024]{0:T(1024)(128)(4,1)} %broadcast_bitcast_fusion) | copy-start | bytes 3076
  386.1 99.5 %copy-start.1 = (bf16[2,224,1024]{2,1,0:T(8,128)(2,1)S(1)}, bf16[2,224,1024]{2,1,0:T(8,128)(2,1)}, u32[]{:S(2)}) copy-start(bf16[2,224,1024]{2,1,0:T(8,128)(2,1)} %param.14) | copy-start | bytes 2752516
Sparse Core Ops, SparseCore 0:
  9.6 70.9 all-gather.5
  83.0 112.2 all-gather.3
  197.6 112.0 all-gather.7
  399.0 86.6 reduce-scatter.1
where the time goes:
time: 493 us; the launch traced here: 492 us
  waiting for transfers between devices  271 us (55%)
  matrix products  128 us (26%)
  local copies, waits for them, and re-layouts  51.4 us (10%)
  loops' own time  18 us (4%)
  between operations  13.3 us (3%)
  other arithmetic  10.7 us (2%)
    all_gather x1, waiting for transfers between devices, local(): lax.all_gather(q_weight, 'dp', axis=1, tiled=True)  115 us
    reduce_scatter x1, waiting for transfers between devices, local(): lax.psum_scatter(jnp.where(row_kinds[:, None] == 1, image_part, text_part...  86.8 us
    all_gather x1, waiting for transfers between devices, local(): lax.all_gather(kv_needed, 'dp', axis=1, tiled=True)  67.9 us
    dot_general x16, matrix products, one_block(): jnp.dot(row_block, lax.dynamic_index_in_dim(shard_piece, block_kind, 0, k...  66.1 us
    sub x2, matrix products, attend(): weights = jnp.exp(scores - row_max)  21.7 us
    unnamed x18, local copies, waits for them, and re-layouts  17.1 us
    another operation x1, loops' own time, project_rows(): products = lax.map(one_block, (blocks, block_kinds))  16.5 us
    dot_general x2, matrix products, attend(): jnp.einsum('gjqk,kgd->qgjd', weights, value_heads, preferred_element_type...  14.8 us
  transfers between devices with their start and end apart: 4, of which 3 were waited for; matrix products, arithmetic and copies ran while one was open for 33% of the time, Pallas kernels for 0%

commit v1 on v0

v1 whole, which is shorter than its diff:
```python
import functools
import math

import jax
import jax.numpy as jnp
import numpy as np
from jax import lax
from jax.experimental import pallas as pl
from jax.experimental.pallas import tpu as pltpu
from jax.sharding import PartitionSpec as P

HD = 128
KVH = 4
QHEADS = 16
BLK = 128
CORES = 2
MESH = pl.DeviceIdType.MESH
NT = (((1,), (1,)), ((), ()))


rope_theta = 1000000.0


def rotary_tables(length, head_width):
    half_width = head_width // 2
    frequency = rope_theta ** (-np.arange(half_width, dtype=np.float32) * 2.0 / head_width)
    angles = np.arange(length, dtype=np.float32)[:, None] * frequency.astype(np.float32)[None, :]
    sines = np.sin(angles)
    return (
        np.concatenate([np.cos(angles)] * 2, axis=1).astype(np.float32),
        np.concatenate([-sines, sines], axis=1).astype(np.float32),
    )


def split_chips(devices):
    chips = devices // CORES
    inner = 1 << (int(math.log2(chips)) // 2)
    return chips // inner, inner


def kernel(
    lines, inner, mps, heads, pairs,
    tok, in_qkv, in_o, kinds, layout, cosine, sine,
    out,
    w_qkv, w_o, acc, queries, keys, values, tok_stage, send_buf, recv_buf, out_stage,
    load_sem, z_sem, x_sem, core_sem, recv_sem, y_send, y_recv, tok_sem, out_sem,
):
    length, width = tok.shape
    plane_cols = width // lines
    slots, shard_rows = w_qkv.shape[2], w_qkv.shape[3]
    part_rows = length // mps
    q_cols = heads * HD
    per_pair = heads // pairs
    row_tile = min(512, length)
    out_tile = min(256, part_rows)

    me = lax.axis_index("dp")
    mp = lax.axis_index("mp")
    core = me % CORES
    x = (me // CORES) % inner
    z = me // (CORES * inner)
    other = 1 - core
    mine = x * CORES + core

    def at(z_, x_, core_):
        return ((z_ * inner + x_) * CORES + core_, mp)

    def order(k):
        picked = jnp.int32(0)
        for place in range(lines):
            ranked = sorted(range(lines), key=lambda p: (abs(p - place), p))
            picked = jnp.where(z == place, ranked[k], picked)
        return picked

    weights = (w_qkv, w_o)

    def send(ph, p, s, m, sem, device):
        block = weights[ph].at[p, m, s]
        return pltpu.make_async_remote_copy(
            src_ref=block, dst_ref=block, send_sem=sem, recv_sem=recv_sem.at[ph, p, s, m],
            device_id=device, device_id_type=MESH,
        )

    def z_copies(ph, p, m):
        up = send(ph, p, mine, m, z_sem.at[ph, 0, p, m], at(z + 1, x, core))
        down = send(ph, p, mine, m, z_sem.at[ph, 1, p, m], at(z - 1, x, core))
        return ((p <= z) & (z < lines - 1), up), ((p >= z) & (z > 0), down)

    def push_z(ph, p, m):
        for condition, copy in z_copies(ph, p, m):
            pl.when(condition)(copy.start)

    def x_copy(ph, p, j, m):
        return send(ph, p, mine, m, x_sem.at[ph, j - 1, p, m], at(z, (x + j) % inner, core))

    def core_copy(ph, p, j, m):
        slot = ((x + j) % inner) * CORES + core
        return send(ph, p, slot, m, core_sem.at[ph, j, p, m], at(z, x, other))

    def push_xc(ph, p, m):
        for j in range(1, inner):
            x_copy(ph, p, j, m).start()
        core_copy(ph, p, 0, m).start()

    def arrived(ph, p, s, m):
        send(ph, p, s, m, core_sem.at[ph, 0, p, m], at(z, x, other)).wait_recv()

    def lane(ph, distance):
        for m in range(2):
            for valid, p in ((z >= distance, z - distance), (z + distance < lines, z + distance)):
                @pl.when(valid)
                def _():
                    arrived(ph, p, mine, m)
                    push_z(ph, p, m)
                    push_xc(ph, p, m)

    def complete(ph, p):
        for m in range(2):
            for j in range(1, inner):
                arrived(ph, p, ((x + j) % inner) * CORES + core, m)
                core_copy(ph, p, j, m).start()
        for m in range(2):
            for j in range(inner):
                arrived(ph, p, j * CORES + other, m)

    def token_copy(k):
        columns = pl.ds(pl.multiple_of(order(k) * plane_cols, 128), plane_cols)
        return pltpu.make_async_copy(tok.at[:, columns], tok_stage, tok_sem.at[k])

    def project(k):
        p = order(k)
        token_copy(k).wait()
        col_tile = min(512, w_qkv.shape[4])
        for c in range(0, w_qkv.shape[4], col_tile):
            @pl.loop(0, length // row_tile)
            def _(i):
                rows = pl.ds(pl.multiple_of(i * row_tile, row_tile), row_tile)
                block = tok_stage[rows, :]
                text = w_qkv[p, 0, :, :, c : c + col_tile].reshape(plane_cols, col_tile)
                image = w_qkv[p, 1, :, :, c : c + col_tile].reshape(plane_cols, col_tile)
                result = jnp.where(
                    kinds[rows, :] == 1,
                    jnp.dot(block, image, preferred_element_type=jnp.float32),
                    jnp.dot(block, text, preferred_element_type=jnp.float32),
                )
                if k == 0:
                    acc[rows, c : c + col_tile] = result
                else:
                    acc[rows, c : c + col_tile] += result
        if k + 1 < lines:
            token_copy(k + 1).start()

    def rope():
        tile = min(256, length)

        @pl.loop(0, length // tile)
        def _(i):
            rows = pl.ds(pl.multiple_of(i * tile, tile), tile)
            cos, sin = cosine[rows, :], sine[rows, :]

            def turned(first):
                part = acc[rows, first : first + HD]
                return (part * cos + pltpu.roll(part, HD // 2, 1) * sin).astype(jnp.bfloat16)

            for h in range(heads):
                queries[rows, h * HD : (h + 1) * HD] = turned(h * HD)
            for g in range(pairs):
                first = q_cols + g * 2 * HD
                keys[rows, g * HD : (g + 1) * HD] = turned(first)
                values[rows, g * HD : (g + 1) * HD] = acc[rows, first + HD : first + 2 * HD].astype(
                    jnp.bfloat16
                )

    def attend(part):
        scale = HD ** (-0.5)
        together = 2 if per_pair % 2 == 0 else 1

        @pl.loop(0, part_rows // BLK)
        def _(i):
            block = part * (part_rows // BLK) + i
            rows = pl.ds(pl.multiple_of(block * BLK, BLK), BLK)
            seen = layout[pl.ds(block, 1), :]
            key_pos = lax.broadcasted_iota(jnp.int32, (BLK, length), 1)
            query_pos = lax.broadcasted_iota(jnp.int32, (BLK, length), 0) + block * BLK
            last = jnp.where(seen == 1, length, jnp.where(seen == 2, 0, -length))
            bias = jnp.where(key_pos <= query_pos + last, 0.0, -1e30)
            for g in range(pairs):
                key, value = keys[:, g * HD : (g + 1) * HD], values[:, g * HD : (g + 1) * HD]
                for first in range(g * per_pair, (g + 1) * per_pair, together):
                    query = jnp.concatenate(
                        [queries[rows, h * HD : (h + 1) * HD] for h in range(first, first + together)],
                        axis=0,
                    )
                    scores = lax.dot_general(query, key, NT, preferred_element_type=jnp.float32)
                    scores = scores.reshape(together, BLK, length) * scale + bias[None]
                    share = jnp.exp(scores - jnp.max(scores, axis=-1, keepdims=True))
                    total = jnp.sum(share, axis=-1, keepdims=True)
                    mixed = jnp.dot(
                        share.astype(jnp.bfloat16).reshape(together * BLK, length),
                        value,
                        preferred_element_type=jnp.float32,
                    ).reshape(together, BLK, HD) / total
                    for h in range(together):
                        queries[rows, (first + h) * HD : (first + h + 1) * HD] = mixed[h].astype(
                            jnp.bfloat16
                        )

    def out_rows(p, first, store):
        @pl.loop(0, part_rows // out_tile)
        def _(i):
            rows = pl.ds(pl.multiple_of(first + i * out_tile, out_tile), out_tile)
            block = queries[rows, :]
            text = w_o[p, 0].reshape(plane_cols, q_cols)
            image = w_o[p, 1].reshape(plane_cols, q_cols)
            result = jnp.where(
                kinds[rows, :] == 1,
                lax.dot_general(block, image, NT, preferred_element_type=jnp.float32),
                lax.dot_general(block, text, NT, preferred_element_type=jnp.float32),
            )
            store(pl.ds(pl.multiple_of(i * out_tile, out_tile), out_tile), result.astype(jnp.bfloat16))

    def y_copy(k, j):
        return pltpu.make_async_remote_copy(
            src_ref=send_buf.at[k, j - 1], dst_ref=recv_buf.at[k, j - 1],
            send_sem=y_send.at[k, j - 1], recv_sem=y_recv.at[k, j - 1],
            device_id=(me, (mp + j) % mps), device_id_type=MESH,
        )

    def give(k):
        for j in range(1, mps):
            def store(rows, result):
                send_buf[k, j - 1, rows, :] = result

            out_rows(order(k), ((mp + j) % mps) * part_rows, store)
            y_copy(k, j).start()

    def out_copy(k):
        columns = pl.ds(pl.multiple_of(order(k) * plane_cols, 128), plane_cols)
        return pltpu.make_async_copy(out_stage.at[k % 2], out.at[:, columns], out_sem.at[k])

    def take(k):
        if k >= 2:
            out_copy(k - 2).wait()
        for j in range(1, mps):
            y_copy(k, j).wait_recv()

        def store(rows, result):
            total = result.astype(jnp.float32)
            for j in range(1, mps):
                total += recv_buf[k, j - 1, rows, :].astype(jnp.float32)
            out_stage[k % 2, rows, :] = total.astype(jnp.bfloat16)

        out_rows(order(k), mp * part_rows, store)
        out_copy(k).start()

    loads = [
        pltpu.make_async_copy(source, target.at[z, :, mine], load_sem.at[i])
        for i, (source, target) in enumerate(((in_qkv, w_qkv), (in_o, w_o)))
    ]
    for load in loads:
        load.start()
    token_copy(0).start()

    barrier = pltpu.get_barrier_semaphore()

    def greet(device):
        pl.semaphore_signal(barrier, inc=1, device_id=device, device_id_type=MESH)

    pl.when(z > 0)(lambda: greet(at(z - 1, x, core)))
    pl.when(z < lines - 1)(lambda: greet(at(z + 1, x, core)))
    for j in range(1, inner):
        greet(at(z, (x + j) % inner, core))
    greet(at(z, x, other))
    for j in range(1, mps):
        greet((me, (mp + j) % mps))
    ends = jnp.where(z > 0, 1, 0) + jnp.where(z < lines - 1, 1, 0)
    pl.semaphore_wait(barrier, inner + mps - 1 + ends)

    loads[0].wait()
    for m in range(2):
        push_z(0, z, m)
        push_xc(0, z, m)
    loads[1].wait()
    for k in range(lines):
        if k + 1 < lines:
            lane(0, k + 1)
        if k == max(lines - 2, 0):
            for m in range(2):
                push_z(1, z, m)
        complete(0, order(k))
        if k == lines - 1:
            for m in range(2):
                push_xc(1, z, m)
        project(k)
    if lines > 1:
        lane(1, 1)
    rope()
    for j in range(1, mps):
        attend((mp + j) % mps)
    if lines > 2:
        lane(1, 2)
    complete(1, order(0))
    give(0)
    attend(mp)
    for distance in range(3, lines):
        lane(1, distance)
    for k in range(1, lines):
        complete(1, order(k))
        give(k)
        take(k - 1)
    take(lines - 1)

    for k in range(max(lines - 2, 0), lines):
        out_copy(k).wait()
    for k in range(lines):
        for j in range(1, mps):
            y_copy(k, j).wait_send()
    for ph in range(2):
        for p in range(lines):
            for m in range(2):
                for condition, copy in z_copies(ph, p, m):
                    pl.when(condition)(copy.wait_send)
                for j in range(1, inner):
                    x_copy(ph, p, j, m).wait_send()
                for j in range(inner):
                    core_copy(ph, p, j, m).wait_send()


def local(devices, mps, tokens, modality, block_mask, q_weight, kv_weight, o_weight):
    states = tokens[0]
    length, width = states.shape
    heads = q_weight.shape[2] // HD
    group_size = QHEADS // KVH
    pairs = max(1, heads // group_size)
    first_pair = lax.axis_index("mp") * heads // group_size
    kv_needed = lax.dynamic_slice_in_dim(kv_weight, first_pair * (2 * HD), pairs * 2 * HD, 2)
    qkv = jnp.concatenate([q_weight, kv_needed], axis=2)
    o_turned = jnp.swapaxes(o_weight, 1, 2)
    kinds = jnp.repeat(modality[0], BLK)[:, None]
    layout = jnp.repeat(block_mask[0], BLK, axis=1)
    cosine, sine = rotary_tables(length, HD)

    lines, inner = split_chips(devices)
    slots = inner * CORES
    plane_cols = width // lines
    part_rows = length // mps
    shard_rows, qkv_cols = qkv.shape[1:]
    bf16, f32 = jnp.bfloat16, jnp.float32
    dma = pltpu.SemaphoreType.DMA
    in_hbm = pl.BlockSpec(memory_space=pltpu.HBM)
    in_vmem = pl.BlockSpec(memory_space=pltpu.VMEM)
    out = pl.pallas_call(
        functools.partial(kernel, lines, inner, mps, heads, pairs),
        out_shape=jax.ShapeDtypeStruct((part_rows, width), bf16),
        in_specs=[in_hbm] * 3 + [in_vmem] * 4,
        out_specs=in_hbm,
        scratch_shapes=[
            pltpu.VMEM((lines, 2, slots, shard_rows, qkv_cols), bf16),
            pltpu.VMEM((lines, 2, slots, shard_rows, heads * HD), bf16),
            pltpu.VMEM((length, qkv_cols), f32),
            pltpu.VMEM((length, heads * HD), bf16),
            pltpu.VMEM((length, pairs * HD), bf16),
            pltpu.VMEM((length, pairs * HD), bf16),
            pltpu.VMEM((length, plane_cols), bf16),
            pltpu.VMEM((lines, mps - 1, part_rows, plane_cols), bf16),
            pltpu.VMEM((lines, mps - 1, part_rows, plane_cols), bf16),
            pltpu.VMEM((2, part_rows, plane_cols), bf16),
            dma((2,)),
            dma((2, 2, lines, 2)),
            dma((2, max(inner - 1, 1), lines, 2)),
            dma((2, inner, lines, 2)),
            dma((2, lines, slots, 2)),
            dma((lines, mps - 1)),
            dma((lines, mps - 1)),
            dma((lines,)),
            dma((lines,)),
        ],
        compiler_params=pltpu.CompilerParams(
            collective_id=0, has_side_effects=True, vmem_limit_bytes=64 * 2**20 - 2**19
        ),
        cost_estimate=pl.CostEstimate(
            flops=4 * length * width * (qkv_cols + heads * HD) + 4 * length * length * heads * HD,
            bytes_accessed=4 * length * width,
            transcendentals=length * length * heads,
        ),
    )(states, qkv, o_turned, kinds, layout, cosine, sine)
    return out[None]


def solution(mesh):
    in_specs = (
        P("dp", None, None),
        P("dp", None),
        P("dp", None, None),
        P(None, "dp", "mp"),
        P(None, "dp", None),
        P(None, "mp", "dp"),
    )
    out_specs = P("dp", "mp", None)
    return jax.shard_map(
        functools.partial(local, mesh.shape["dp"], mesh.shape["mp"]),
        mesh=mesh, in_specs=in_specs, out_specs=out_specs, check_vma=False,
    )
```

time: 493 us -> 257 us (0.52)
  waiting for transfers between devices: 271 us -> 0 us
  Pallas kernels: 0 us -> 246 us
  matrix products: 128 us -> 0 us
  local copies, waits for them, and re-layouts: 51.4 us -> 8.36 us
  loops' own time: 18 us -> 0 us
  between operations: 13.3 us -> 0.02 us
  other arithmetic: 10.7 us -> 2.34 us
    pallas_call x0 -> x1, Pallas kernels: none -> 246 us  [local(): pl.pallas_call(functools.partial(kernel, lines, inner, mps, heads, pairs)...]
    all_gather x3 -> x0, waiting for transfers between devices: 182 us -> none  [the longest x1 115 us: local(): lax.all_gather(q_weight, 'dp', axis=1, tiled=True)]
    dot_general x20 -> x0, matrix products: 106 us -> none  [the longest x16 66.1 us: one_block(): jnp.dot(row_block, lax.dynamic_index_in_dim(shard_piece, block_kind, 0, k...]
    reduce_scatter x1 -> x0, waiting for transfers between devices: 86.8 us -> none  [local(): lax.psum_scatter(jnp.where(row_kinds[:, None] == 1, image_part, text_part...]
    sub x2 -> x0, matrix products: 21.7 us -> none  [attend(): weights = jnp.exp(scores - row_max)]
    another operation x2 -> x0, loops' own time: 18 us -> none  [the longest x1 16.5 us: project_rows(): products = lax.map(one_block, (blocks, block_kinds))]
    unnamed x18 -> x1, local copies, waits for them, and re-layouts: 17.1 us -> 4.11 us
    reshape x3 -> x1, local copies, waits for them, and re-layouts: 13.4 us -> 0.68 us  [local(): layout = jnp.repeat(block_mask[0], BLK, axis=1)]
  transfers between devices with their start and end apart: 4 -> 0, of which waited for: 3 -> 0; matrix products, arithmetic and copies ran while one was open for 33% -> 0% of each run, Pallas kernels for 0% -> 0%
where the time goes in v1:
time: 257 us
  Pallas kernels  246 us (96%)
  local copies, waits for them, and re-layouts  8.36 us (3%)
    pallas_call x1, Pallas kernels, local(): pl.pallas_call(functools.partial(kernel, lines, inner, mps, heads, pairs)...  246 us

profile of v1, /device:TPU:0, one launch (start us, length us, event | category | flops | bytes accessed | tf_op | source)
XLA Modules:
  0.0 257.1 jit_solution(3264587437019775197)
XLA Ops:
  0.0 0.7 broadcast_in_dim.9
  0.7 0.8 copy.10
  1.5 0.7 broadcast_bitcast_fusion.layout
  2.2 1.0 constant_dynamic-slice_fusion
  3.2 1.0 copy.11.kinds
  4.3 2.3 pad_maximum_fusion.in_qkv
  6.6 246.4 %shard_map.82 = bf16[512,3584]{1,0:T(8,128)(2,1)} custom-call(bf16[1024,3584]{1,0:T(8,128)(2,1)} %bitcast.12, bf16[2,224,1536]{2,1,0:T(8,128)(2,1)} %pad_maximum_fusion.in_qkv, bf16[2,224,1024]{2,1,0:T(8,128)(2,1)} %bitcast.13, s32[1024,1]{1,0:T(8,128)} %copy.11.kinds, s32[8,1024]{1,0:T(8,128)} %broadcast_bitcast_fusion.layout, ...), custom_call_target="tpu_custom_call" | custom-call | flops 41875931136 | bytes 14680064 | tf_op jit(solution)/shard_map/pallas_call | solution.py:352
  253.0 4.1 %copy.13 = bf16[1,512,3584]{2,1,0:T(8,128)(2,1)} copy(bf16[1,512,3584]{2,1,0:T(8,128)(2,1)} %bitcast.8) | data formatting | bytes 7340032

commit v2 on v1

--- a/solution.py
+++ b/solution.py
@@ -40,10 +40,10 @@
 
 def kernel(
     lines, inner, mps, heads, pairs,
-    tok, in_qkv, in_o, kinds, layout, cosine, sine,
+    tok, in_q, in_kv, in_o, modality, block_mask, cosine, sine,
     out,
-    w_qkv, w_o, acc, queries, keys, values, tok_stage, send_buf, recv_buf, out_stage,
-    load_sem, z_sem, x_sem, core_sem, recv_sem, y_send, y_recv, tok_sem, out_sem,
+    kinds, layout, w_qkv, w_o, acc, queries, keys, values, tok_stage, send_buf, recv_buf, out_stage,
+    load_sem, z_sem, x_sem, turn_sem, core_sem, recv_sem, y_send, y_recv, tok_sem, out_sem,
 ):
     length, width = tok.shape
     plane_cols = width // lines
@@ -97,10 +97,38 @@
         slot = ((x + j) % inner) * CORES + core
         return send(ph, p, slot, m, core_sem.at[ph, j, p, m], at(z, x, other))
 
+    def ends(p):
+        return (p == 0) | (p == lines - 1)
+
+    def takes_x(p, m):
+        return (p == z) | jnp.logical_not(ends(p)) if m == 0 else p >= 0
+
     def push_xc(ph, p, m):
-        for j in range(1, inner):
-            x_copy(ph, p, j, m).start()
+        @pl.when(takes_x(p, m))
+        def _():
+            for j in range(1, inner):
+                x_copy(ph, p, j, m).start()
+
         core_copy(ph, p, 0, m).start()
+
+    def turn_copies(ph, p, j):
+        slot = ((x + j) % inner) * CORES + core
+        up = send(ph, p, slot, 0, turn_sem.at[ph, 0, p, j - 1], at(z + 1, x, core))
+        down = send(ph, p, slot, 0, turn_sem.at[ph, 1, p, j - 1], at(z - 1, x, core))
+        return ((p == 0) & (z < lines - 1), up), ((p == lines - 1) & (z > 0), down)
+
+    def push_turn(ph, p, j):
+        for condition, copy in turn_copies(ph, p, j):
+            pl.when(condition)(copy.start)
+
+    def turn(ph, distance):
+        for valid, p in ((z == distance, 0), (z + distance == lines - 1, lines - 1)):
+            @pl.when(valid)
+            def _():
+                for j in range(1, inner):
+                    arrived(ph, p, ((x + j) % inner) * CORES + core, 0)
+                    push_turn(ph, p, j)
+                    core_copy(ph, p, j, 0).start()
 
     def arrived(ph, p, s, m):
         send(ph, p, s, m, core_sem.at[ph, 0, p, m], at(z, x, other)).wait_recv()
@@ -116,9 +144,14 @@
 
     def complete(ph, p):
         for m in range(2):
-            for j in range(1, inner):
-                arrived(ph, p, ((x + j) % inner) * CORES + core, m)
-                core_copy(ph, p, j, m).start()
+            @pl.when(takes_x(p, m))
+            def _():
+                for j in range(1, inner):
+                    arrived(ph, p, ((x + j) % inner) * CORES + core, m)
+                    if m == 0:
+                        pl.when(p == z)(lambda: push_turn(ph, p, j))
+                    core_copy(ph, p, j, m).start()
+
         for m in range(2):
             for j in range(inner):
                 arrived(ph, p, j * CORES + other, m)
@@ -171,11 +204,11 @@
                     jnp.bfloat16
                 )
 
-    def attend(part):
+    def attend(part, start, stop):
         scale = HD ** (-0.5)
         together = 2 if per_pair % 2 == 0 else 1
 
-        @pl.loop(0, part_rows // BLK)
+        @pl.loop(start, stop)
         def _(i):
             block = part * (part_rows // BLK) + i
             rows = pl.ds(pl.multiple_of(block * BLK, BLK), BLK)
@@ -253,9 +286,13 @@
         out_rows(order(k), mp * part_rows, store)
         out_copy(k).start()
 
+    pair_cols = pairs * 2 * HD
+    first_pair = (mp * heads // (QHEADS // KVH)) * (2 * HD)
+    kv_part = in_kv.at[:, :, pl.ds(pl.multiple_of(first_pair, 2 * HD), pair_cols)]
     loads = [
-        pltpu.make_async_copy(source, target.at[z, :, mine], load_sem.at[i])
-        for i, (source, target) in enumerate(((in_qkv, w_qkv), (in_o, w_o)))
+        pltpu.make_async_copy(in_q, w_qkv.at[z, :, mine, :, pl.ds(0, q_cols)], load_sem.at[0]),
+        pltpu.make_async_copy(kv_part, w_qkv.at[z, :, mine, :, pl.ds(q_cols, pair_cols)], load_sem.at[1]),
+        pltpu.make_async_copy(in_o, w_o.at[z, :, mine], load_sem.at[2]),
     ]
     for load in loads:
         load.start()
@@ -273,15 +310,23 @@
     greet(at(z, x, other))
     for j in range(1, mps):
         greet((me, (mp + j) % mps))
-    ends = jnp.where(z > 0, 1, 0) + jnp.where(z < lines - 1, 1, 0)
-    pl.semaphore_wait(barrier, inner + mps - 1 + ends)
+    along = jnp.where(z > 0, 1, 0) + jnp.where(z < lines - 1, 1, 0)
+    pl.semaphore_wait(barrier, inner + mps - 1 + along)
 
     loads[0].wait()
+    loads[1].wait()
     for m in range(2):
         push_z(0, z, m)
         push_xc(0, z, m)
-    loads[1].wait()
+    loads[2].wait()
+    blocks = length // BLK
+    for i in range(blocks):
+        kinds[i * BLK : (i + 1) * BLK, :] = jnp.full((BLK, 1), modality[0, i], jnp.int32)
+        for j in range(blocks):
+            layout[i : i + 1, j * BLK : (j + 1) * BLK] = jnp.full((1, BLK), block_mask[i, j], jnp.int32)
     for k in range(lines):
+        if k > 0:
+            turn(0, k)
         if k + 1 < lines:
             lane(0, k + 1)
         if k == max(lines - 2, 0):
@@ -295,16 +340,22 @@
     if lines > 1:
         lane(1, 1)
     rope()
+    part_blocks = part_rows // BLK
     for j in range(1, mps):
-        attend((mp + j) % mps)
+        attend((mp + j) % mps, 0, part_blocks)
+    complete(1, order(0))
     if lines > 2:
         lane(1, 2)
-    complete(1, order(0))
     give(0)
-    attend(mp)
-    for distance in range(3, lines):
-        lane(1, distance)
+    attend(mp, 0, part_blocks // 2)
+    if lines > 1:
+        turn(1, 1)
+    attend(mp, part_blocks // 2, part_blocks)
     for k in range(1, lines):
+        if k > 1:
+            turn(1, k)
+        if k + 2 <= lines - 1:
+            lane(1, k + 2)
         complete(1, order(k))
         give(k)
         take(k - 1)
@@ -320,10 +371,17 @@
             for m in range(2):
                 for condition, copy in z_copies(ph, p, m):
                     pl.when(condition)(copy.wait_send)
-                for j in range(1, inner):
-                    x_copy(ph, p, j, m).wait_send()
+                @pl.when(takes_x(p, m))
+                def _():
+                    for j in range(1, inner):
+                        x_copy(ph, p, j, m).wait_send()
+
                 for j in range(inner):
                     core_copy(ph, p, j, m).wait_send()
+            if p in (0, lines - 1):
+                for j in range(1, inner):
+                    for condition, copy in turn_copies(ph, p, j):
+                        pl.when(condition)(copy.wait_send)
 
 
 def local(devices, mps, tokens, modality, block_mask, q_weight, kv_weight, o_weight):
@@ -332,29 +390,27 @@
     heads = q_weight.shape[2] // HD
     group_size = QHEADS // KVH
     pairs = max(1, heads // group_size)
-    first_pair = lax.axis_index("mp") * heads // group_size
-    kv_needed = lax.dynamic_slice_in_dim(kv_weight, first_pair * (2 * HD), pairs * 2 * HD, 2)
-    qkv = jnp.concatenate([q_weight, kv_needed], axis=2)
     o_turned = jnp.swapaxes(o_weight, 1, 2)
-    kinds = jnp.repeat(modality[0], BLK)[:, None]
-    layout = jnp.repeat(block_mask[0], BLK, axis=1)
     cosine, sine = rotary_tables(length, HD)
 
     lines, inner = split_chips(devices)
     slots = inner * CORES
     plane_cols = width // lines
     part_rows = length // mps
-    shard_rows, qkv_cols = qkv.shape[1:]
+    shard_rows, qkv_cols = q_weight.shape[1], (heads + 2 * pairs) * HD
     bf16, f32 = jnp.bfloat16, jnp.float32
     dma = pltpu.SemaphoreType.DMA
     in_hbm = pl.BlockSpec(memory_space=pltpu.HBM)
     in_vmem = pl.BlockSpec(memory_space=pltpu.VMEM)
+    in_smem = pl.BlockSpec(memory_space=pltpu.SMEM)
     out = pl.pallas_call(
         functools.partial(kernel, lines, inner, mps, heads, pairs),
         out_shape=jax.ShapeDtypeStruct((part_rows, width), bf16),
-        in_specs=[in_hbm] * 3 + [in_vmem] * 4,
+        in_specs=[in_hbm] * 4 + [in_smem] * 2 + [in_vmem] * 2,
         out_specs=in_hbm,
         scratch_shapes=[
+            pltpu.VMEM((length, 1), jnp.int32),
+            pltpu.VMEM((length // BLK, length), jnp.int32),
             pltpu.VMEM((lines, 2, slots, shard_rows, qkv_cols), bf16),
             pltpu.VMEM((lines, 2, slots, shard_rows, heads * HD), bf16),
             pltpu.VMEM((length, qkv_cols), f32),
@@ -365,9 +421,10 @@
             pltpu.VMEM((lines, mps - 1, part_rows, plane_cols), bf16),
             pltpu.VMEM((lines, mps - 1, part_rows, plane_cols), bf16),
             pltpu.VMEM((2, part_rows, plane_cols), bf16),
-            dma((2,)),
+            dma((3,)),
             dma((2, 2, lines, 2)),
             dma((2, max(inner - 1, 1), lines, 2)),
+            dma((2, 2, lines, max(inner - 1, 1))),
             dma((2, inner, lines, 2)),
             dma((2, lines, slots, 2)),
             dma((lines, mps - 1)),
@@ -383,7 +440,7 @@
             bytes_accessed=4 * length * width,
             transcendentals=length * length * heads,
         ),
-    )(states, qkv, o_turned, kinds, layout, cosine, sine)
+    )(states, q_weight, kv_weight, o_turned, modality, block_mask[0], cosine, sine)
     return out[None]
 
 

time: 257 us -> 244 us (0.949)
  Pallas kernels: 246 us -> 238 us
  local copies, waits for them, and re-layouts: 8.36 us -> 4.11 us
    pallas_call x1, Pallas kernels: 246 us -> 238 us  [local(): pl.pallas_call(functools.partial(kernel, lines, inner, mps, heads, pairs)...]
where the time goes in v2:
time: 244 us; the launch traced here: 242 us
  Pallas kernels  238 us (98%)
  local copies, waits for them, and re-layouts  4.11 us (2%)
    pallas_call x1, Pallas kernels, local(): pl.pallas_call(functools.partial(kernel, lines, inner, mps, heads, pairs)...  238 us

profile of v2, /device:TPU:0, one launch (start us, length us, event | category | flops | bytes accessed | tf_op | source)
XLA Modules:
  0.0 242.0 jit_solution(17600231175512449851)
XLA Ops:
  0.0 237.9 %shard_map.82 = bf16[512,3584]{1,0:T(8,128)(2,1)} custom-call(bf16[1024,3584]{1,0:T(8,128)(2,1)} %bitcast.5, bf16[2,224,1024]{2,1,0:T(8,128)(2,1)} %in_q.1, bf16[2,224,1024]{2,1,0:T(8,128)(2,1)} %in_kv.1, bf16[2,224,1024]{2,1,0:T(8,128)(2,1)} %bitcast.6, s32[1,8]{1,0:T(1,128)} %modality.1, s32[8,8]{1,0:T(8,128)} %bitcast.7, ...), custom_call_target="tpu_custom_call" | custom-call | flops 41875931136 | bytes 14680064 | tf_op jit(solution)/shard_map/pallas_call | solution.py:406
  237.9 4.1 %copy.10 = bf16[1,512,3584]{2,1,0:T(8,128)(2,1)} copy(bf16[1,512,3584]{2,1,0:T(8,128)(2,1)} %bitcast.4) | data formatting | bytes 7340032
